TPU v7x, 512 devices: a whole 4x8x8 slice. The times are simulated.
512 devices in a mesh: dp: 4 (over x), expert: 128 (over y, z, core).
Axes of the slice: x: 4, y: 8, z: 8, core: 2. Of those that a mesh axis runs over, the one named last changes fastest.
Arguments:
- out_grad: bfloat16 [8192, 1536], P(('dp', 'expert')), may hold values from -1.5 to 1.5
- routes: int32 [8192, 8], P(('dp', 'expert')), may hold values from 0 to 127, all different within a row; in each aligned block of 16 rows (0 to 15, 16 to 31, ...) at most 2 rows name the same one
- gate_probs: float32 [8192, 8], P(('dp', 'expert')), may hold values from 0.05 to 1
- saved_inputs: bfloat16 [4, 128, 256, 1536], P('dp', 'expert'), may hold values from -6 to 6
- w_gate: bfloat16 [128, 1536, 384], P('expert', 'dp'), may hold values from -0.15625 to 0.15625
- w_up: bfloat16 [128, 1536, 384], P('expert', 'dp'), may hold values from -0.15625 to 0.15625
- w_down: bfloat16 [128, 1536, 384], P('expert', 'dp'), may hold values from -0.3125 to 0.3125
Outputs:
- token_grad: bfloat16 [8192, 1536], P(('dp', 'expert'))
- prob_grad: float32 [8192, 8], P(('dp', 'expert'))
- grad_gate: bfloat16 [128, 1536, 384], P('expert', 'dp')
- grad_up: bfloat16 [128, 1536, 384], P('expert', 'dp')
- grad_down: bfloat16 [128, 1536, 384], P('expert', 'dp')
Inputs may be any that keep to these rules, and one draw needn't show every extreme that they name: `routes`: within the tokens of one device no expert is named by more than 2 entries, a bound that some block reaches; a token names 8 different experts.
All inputs are finite; a program needn't handle non-finite values.
Results may differ from a plain program's by a relative error of at most 0.02.
Values may be sent and summed in bfloat16 or wider, within the bound.
No kernel may reach another device: no remote copies, remote signals or barrier semaphores. Data moves between devices by JAX's collectives and lax.ppermute only.
A program may use at most 64 MiB of HBM per device.

v0:
```python
import jax
import jax.numpy as jnp
from jax import lax
from jax.sharding import PartitionSpec as P

TOP = 8


def expert_rows(inputs_rows, grad_rows, prob, gate_w, up_w, down_w):
    pre_gate = jnp.dot(inputs_rows, gate_w, preferred_element_type=jnp.float32)
    pre_up = jnp.dot(inputs_rows, up_w, preferred_element_type=jnp.float32)
    sigma_g = jax.nn.sigmoid(pre_gate)
    activated = pre_gate * sigma_g
    hidden = activated * pre_up
    dh_raw = jnp.dot(grad_rows, down_w, preferred_element_type=jnp.float32)
    row_prob = jnp.sum(hidden * dh_raw, axis=1)
    scaled_hidden = (prob[:, None] * hidden).astype(jnp.bfloat16)
    dh_full = prob[:, None] * dh_raw
    d_up = (dh_full * activated).astype(jnp.bfloat16)
    d_gate = (dh_full * pre_up * sigma_g * (1.0 + pre_gate * (1.0 - sigma_g))).astype(jnp.bfloat16)
    row_grad = (
        jnp.dot(d_gate, gate_w.T, preferred_element_type=jnp.float32)
        + jnp.dot(d_up, up_w.T, preferred_element_type=jnp.float32)
    ).astype(jnp.bfloat16)
    return (row_grad, row_prob, d_gate, d_up, scaled_hidden)


def shards(out_grad, routes, gate_probs, saved_inputs, w_gate, w_up, w_down):
    tok_rows = out_grad.shape[0]
    width = out_grad.shape[1]
    experts_here = lax.axis_size("expert")
    capacity = saved_inputs.shape[2] // experts_here
    all_slots = saved_inputs.shape[2]
    flat_routes = routes.reshape(-1)
    onehot = (flat_routes[:, None] == jnp.arange(experts_here, dtype=jnp.int32)[None, :]).astype(
        jnp.int32
    )
    running = jnp.cumsum(onehot, axis=0)
    slot_of = jnp.sum(onehot * (running - 1), axis=1)
    target = flat_routes * capacity + slot_of
    repeated = jnp.repeat(out_grad, TOP, axis=0)
    send_rows = jnp.zeros((all_slots, width), jnp.bfloat16).at[target].set(repeated)
    send_prob = jnp.zeros((all_slots,), jnp.float32).at[target].set(gate_probs.reshape(-1))
    send_rows = send_rows.reshape(experts_here, capacity, width)
    send_prob = send_prob.reshape(experts_here, capacity)
    recv_rows, recv_prob = (
        lax.all_to_all(send_rows, "expert", split_axis=0, concat_axis=0, tiled=True),
        lax.all_to_all(
            send_prob.astype(jnp.bfloat16), "expert", split_axis=0, concat_axis=0, tiled=True
        ).astype(send_prob.dtype),
    )
    gathered = (
        lax.all_gather(w_gate, "dp", axis=1, tiled=True),
        lax.all_gather(w_up, "dp", axis=1, tiled=True),
        lax.all_gather(w_down, "dp", axis=1, tiled=True),
    )
    gate_w = gathered[0][0]
    up_w = gathered[1][0]
    down_w = gathered[2][0]
    inputs_rows = saved_inputs[0, 0]
    grad_rows = recv_rows.reshape(all_slots, width)
    prob_rows = recv_prob.reshape(all_slots)
    row_grad, row_prob, d_gate, d_up, scaled_hidden = expert_rows(
        inputs_rows, grad_rows, prob_rows, gate_w, up_w, down_w
    )
    part_gate = jnp.dot(inputs_rows.T, d_gate, preferred_element_type=jnp.float32)
    part_up = jnp.dot(inputs_rows.T, d_up, preferred_element_type=jnp.float32)
    part_down = jnp.dot(grad_rows.T, scaled_hidden, preferred_element_type=jnp.float32)
    back_rows, back_prob = (
        lax.all_to_all(
            row_grad.reshape(experts_here, capacity, width),
            "expert",
            split_axis=0,
            concat_axis=0,
            tiled=True,
        ),
        lax.all_to_all(
            row_prob.reshape(experts_here, capacity).astype(jnp.bfloat16),
            "expert",
            split_axis=0,
            concat_axis=0,
            tiled=True,
        ).astype(jnp.float32),
    )
    pair_rows = back_rows.reshape(all_slots, width)[target]
    token_grad = jnp.sum(
        pair_rows.reshape(tok_rows, TOP, width).astype(jnp.float32), axis=1
    ).astype(jnp.bfloat16)
    prob_grad = back_prob.reshape(all_slots)[target].reshape(tok_rows, TOP)
    summed = (
        lax.psum_scatter(
            part_gate[None].astype(jnp.bfloat16), "dp", scatter_dimension=1, tiled=True
        ).astype(jnp.float32),
        lax.psum_scatter(
            part_up[None].astype(jnp.bfloat16), "dp", scatter_dimension=1, tiled=True
        ).astype(jnp.float32),
        lax.psum_scatter(
            part_down[None].astype(jnp.bfloat16), "dp", scatter_dimension=1, tiled=True
        ).astype(jnp.float32),
    )
    grad_gate = summed[0].astype(jnp.bfloat16)
    grad_up = summed[1].astype(jnp.bfloat16)
    grad_down = summed[2].astype(jnp.bfloat16)
    return (token_grad, prob_grad, grad_gate, grad_up, grad_down)


def solution(mesh):
    return jax.shard_map(
        shards,
        mesh=mesh,
        in_specs=(
            P(("dp", "expert"), None),
            P(("dp", "expert"), None),
            P(("dp", "expert"), None),
            P("dp", "expert", None, None),
            P("expert", "dp", None),
            P("expert", "dp", None),
            P("expert", "dp", None),
        ),
        out_specs=(
            P(("dp", "expert"), None),
            P(("dp", "expert"), None),
            P("expert", "dp", None),
            P("expert", "dp", None),
            P("expert", "dp", None),
        ),
        check_vma=False,
    )
```

profile of v0, /device:TPU:8, one launch (start us, length us, event | category | flops | bytes accessed | tf_op | source)
XLA Modules:
  0.0 222.0 jit_solution(12283877655016537545)
XLA Ops:
  11.7 1.0 scatter_custom_fusion
  12.7 0.8 convert_element_type.113
  13.5 17.4 %all-to-all-start = ((bf16[128,1,2]{2,1,0:T(2,128)(2,1)}), bf16[128,1,2]{2,1,0:T(2,128)(2,1)S(1)}, u32[]{:S(2)}, u32[]{:S(2)}) async-start(bf16[128,1,2]{2,1,0:T(2,128)(2,1)} %convert_element_type.113), calls=%async_computation | async-start | bytes 131072 | tf_op jit(solution)/shard_map/all_to_all | solution.py:48
  30.9 1.7 scatter_custom_fusion.1
  32.6 1.2 reshape.108
  33.8 7.9 %all-to-all-done = bf16[128,1,2]{2,1,0:T(2,128)(2,1)S(1)} async-done(((bf16[128,1,2]{2,1,0:T(2,128)(2,1)}), bf16[128,1,2]{2,1,0:T(2,128)(2,1)S(1)}, u32[]{:S(2)}, u32[]{:S(2)}) %all-to-all-start) | async-done | bytes 544 | tf_op jit(solution)/shard_map/all_to_all | solution.py:48
  41.6 6.5 %all-to-all-start.1 = ((bf16[128,2,1536]{2,1,0:T(2,128)(2,1)}), bf16[128,2,1536]{2,1,0:T(2,128)(2,1)S(1)}, u32[]{:S(2)}, u32[]{:S(2)}) async-start(bf16[128,2,1536]{2,1,0:T(2,128)(2,1)} %reshape.108), calls=%async_computation.1 | async-start | bytes 1572864 | tf_op jit(solution)/shard_map/all_to_all | solution.py:47
  49.3 24.8 %all-to-all-done.1 = bf16[128,2,1536]{2,1,0:T(2,128)(2,1)S(1)} async-done(((bf16[128,2,1536]{2,1,0:T(2,128)(2,1)}), bf16[128,2,1536]{2,1,0:T(2,128)(2,1)S(1)}, u32[]{:S(2)}, u32[]{:S(2)}) %all-to-all-start.1) | async-done | bytes 786464 | tf_op jit(solution)/shard_map/all_to_all | solution.py:47
  74.4 2.1 fusion.6
  76.9 1.8 fusion.9
  78.8 30.6 %all-gather.4.cloned.1.call-done = bf16[1,1536,384]{2,1,0:T(8,128)(2,1)} async-done(((bf16[1,384,384]{2,1,0:T(8,128)(2,1)}), bf16[1,1536,384]{2,1,0:T(8,128)(2,1)}) %all-gather.4.cloned.1.call-update) | async-done | bytes 1179664 | tf_op jit(solution)/shard_map/all_gather | solution.py:55
  109.4 2.0 multiply_reduce_fusion
  111.5 1.5 fusion.1
  113.0 6.3 %copy.32 = bf16[1,1536,384]{2,0,1:T(2,128)(2,1)S(1)} copy(bf16[1,1536,384]{1,2,0:T(8,128)(2,1)} %fusion.1) | data formatting | bytes 2359296
  119.3 1.2 copy.43
  120.6 1.5 fusion.2
  122.1 6.3 %copy.34 = bf16[1,1536,384]{2,0,1:T(2,128)(2,1)S(1)} copy(bf16[1,1536,384]{1,2,0:T(8,128)(2,1)} %fusion.2) | data formatting | bytes 2359296
  128.4 1.2 copy.42
  129.6 0.8 convert_element_type.114
  130.4 14.2 %all-to-all-start.3 = ((bf16[128,1,2]{2,1,0:T(2,128)(2,1)}), bf16[128,1,2]{2,1,0:T(2,128)(2,1)S(1)}, u32[]{:S(2)}, u32[]{:S(2)}) async-start(bf16[128,1,2]{2,1,0:T(2,128)(2,1)} %convert_element_type.114), calls=%async_computation.3 | async-start | bytes 131072 | tf_op jit(solution)/shard_map/all_to_all | solution.py:77
  144.6 2.7 %fusion.3 = bf16[1,1536,384]{2,1,0:T(8,128)(2,1)} fusion(bf16[256,1536]{1,0:T(8,128)(2,1)S(1)} %copy-done.4, f32[256]{0:T(256)S(1)} %reshape.114, f32[256,384]{1,0:T(8,128)} %copy-done.7, f32[256,384]{1,0:T(8,128)S(1)} %copy-done.6), kind=kOutput, calls=%fused_computation.11 | convolution fusion | flops 303267840 | bytes 2753536 | tf_op jit(solution)/shard_map/dot_general | solution.py:68
  147.4 1.3 copy-done.2
  150.6 1.2 reshape.110
  151.7 3.6 %all-to-all-done.3 = bf16[128,1,2]{2,1,0:T(2,128)(2,1)S(1)} async-done(((bf16[128,1,2]{2,1,0:T(2,128)(2,1)}), bf16[128,1,2]{2,1,0:T(2,128)(2,1)S(1)}, u32[]{:S(2)}, u32[]{:S(2)}) %all-to-all-start.3) | async-done | bytes 544 | tf_op jit(solution)/shard_map/all_to_all | solution.py:77
  155.3 10.1 %all-to-all-start.2 = ((bf16[128,2,1536]{2,1,0:T(2,128)(2,1)}), bf16[128,2,1536]{2,1,0:T(2,128)(2,1)S(1)}, u32[]{:S(2)}, u32[]{:S(2)}) async-start(bf16[128,2,1536]{2,1,0:T(2,128)(2,1)} %reshape.110), calls=%async_computation.2 | async-start | bytes 1572864 | tf_op jit(solution)/shard_map/all_to_all | solution.py:70
  165.8 1.3 gather_fusion.1
  167.8 23.5 %all-to-all-done.2 = bf16[128,2,1536]{2,1,0:T(2,128)(2,1)S(1)} async-done(((bf16[128,2,1536]{2,1,0:T(2,128)(2,1)}), bf16[128,2,1536]{2,1,0:T(2,128)(2,1)S(1)}, u32[]{:S(2)}, u32[]{:S(2)}) %all-to-all-start.2) | async-done | bytes 786464 | tf_op jit(solution)/shard_map/all_to_all | solution.py:70
  191.6 0.9 gather_fusion
  192.5 0.9 bitcast_reduce_fusion
  193.4 1.3 reshape_bitcast_fusion.1
  195.4 1.3 reshape_bitcast_fusion
  197.5 17.7 %reduce-scatter.8.cloned.1.call-done = bf16[1,384,384]{2,1,0:T(8,128)(2,1)} async-done(((bf16[1,1536,384]{2,1,0:T(8,128)(2,1)}), bf16[1,384,384]{2,1,0:T(8,128)(2,1)}) %reduce-scatter.8.cloned.1.call-update) | async-done | bytes 294928 | tf_op jit(solution)/shard_map/reduce_scatter | solution.py:97
  (56 shorter events, 11.2 us)
Async XLA Ops:
  7.2 67.2 %copy-start = (bf16[1,1,256,1536]{3,2,1,0:T(8,128)(2,1)S(1)}, bf16[1,1,256,1536]{3,2,1,0:T(8,128)(2,1)}, u32[]{:S(2)}) copy-start(bf16[1,1,256,1536]{3,2,1,0:T(8,128)(2,1)} %param.10) | copy-start | bytes 2359300
  7.2 67.2 %all-gather.8.cloned.1.call-start = ((), (), s32[]{:S(2)}) async-start(), calls=%async_computation.9 | async-start | bytes 1474560 | tf_op jit(solution)/shard_map/all_gather | solution.py:53
  7.9 69.0 %all-gather.6.cloned.1.call-start = ((), (), s32[]{:S(2)}) async-start(), calls=%async_computation.8 | async-start | bytes 1474560 | tf_op jit(solution)/shard_map/all_gather | solution.py:54
  13.5 28.2 %all-to-all-start = ((bf16[128,1,2]{2,1,0:T(2,128)(2,1)}), bf16[128,1,2]{2,1,0:T(2,128)(2,1)S(1)}, u32[]{:S(2)}, u32[]{:S(2)}) async-start(bf16[128,1,2]{2,1,0:T(2,128)(2,1)} %convert_element_type.113), calls=%async_computation | async-start | bytes 131072 | tf_op jit(solution)/shard_map/all_to_all | solution.py:48
  41.6 32.4 %all-to-all-start.1 = ((bf16[128,2,1536]{2,1,0:T(2,128)(2,1)}), bf16[128,2,1536]{2,1,0:T(2,128)(2,1)S(1)}, u32[]{:S(2)}, u32[]{:S(2)}) async-start(bf16[128,2,1536]{2,1,0:T(2,128)(2,1)} %reshape.108), calls=%async_computation.1 | async-start | bytes 1572864 | tf_op jit(solution)/shard_map/all_to_all | solution.py:47
  48.1 61.3 %all-gather.4.cloned.1.call-start = ((), (), s32[]{:S(2)}) async-start(), calls=%async_computation.7 | async-start | bytes 1474560 | tf_op jit(solution)/shard_map/all_gather | solution.py:55
  48.9 144.5 %reduce-scatter.10.cloned.1.call-start = ((), (), s32[]{:S(2)}) async-start(), calls=%async_computation.11 | async-start | bytes 1474560
  74.3 35.1 %copy-start.3 = (bf16[256,1536]{1,0:T(8,128)(2,1)}, bf16[256,1536]{1,0:T(8,128)(2,1)S(1)}, u32[]{:S(2)}) copy-start(bf16[256,1536]{1,0:T(8,128)(2,1)S(1)} %reshape.109) | copy-start | bytes 2359300
  76.5 35.0 %copy-start.5 = (f32[256,384]{1,0:T(8,128)}, f32[256,384]{1,0:T(8,128)S(1)}, u32[]{:S(2)}) copy-start(f32[256,384]{1,0:T(8,128)S(1)} %fusion.6) | copy-start | bytes 1179652
  78.8 32.7 %copy-start.7 = (f32[256,384]{1,0:T(8,128)}, f32[256,384]{1,0:T(8,128)S(1)}, u32[]{:S(2)}) copy-start(f32[256,384]{1,0:T(8,128)S(1)} %fusion.9) | copy-start | bytes 1179652
  120.5 74.9 %reduce-scatter.12.cloned.1.call-start = ((), (), s32[]{:S(2)}) async-start(), calls=%async_computation.12 | async-start | bytes 1474560
  129.6 15.0 %copy-start.4 = (bf16[256,1536]{1,0:T(8,128)(2,1)S(1)}, bf16[256,1536]{1,0:T(8,128)(2,1)}, u32[]{:S(2)}) copy-start(bf16[256,1536]{1,0:T(8,128)(2,1)} %copy-done.3) | copy-start | bytes 2359300
  129.6 15.1 %copy-start.6 = (f32[256,384]{1,0:T(8,128)S(1)}, f32[256,384]{1,0:T(8,128)}, u32[]{:S(2)}) copy-start(f32[256,384]{1,0:T(8,128)} %copy-done.5) | copy-start | bytes 1179652
  130.4 24.9 %all-to-all-start.3 = ((bf16[128,1,2]{2,1,0:T(2,128)(2,1)}), bf16[128,1,2]{2,1,0:T(2,128)(2,1)S(1)}, u32[]{:S(2)}, u32[]{:S(2)}) async-start(bf16[128,1,2]{2,1,0:T(2,128)(2,1)} %convert_element_type.114), calls=%async_computation.3 | async-start | bytes 131072 | tf_op jit(solution)/shard_map/all_to_all | solution.py:77
  144.6 70.6 %reduce-scatter.8.cloned.1.call-start = ((), (), s32[]{:S(2)}) async-start(), calls=%async_computation.10 | async-start | bytes 1474560 | tf_op jit(solution)/shard_map/reduce_scatter | solution.py:97
  147.4 1.3 copy-start.2
  148.7 1.3 copy-start.1
  155.3 36.0 %all-to-all-start.2 = ((bf16[128,2,1536]{2,1,0:T(2,128)(2,1)}), bf16[128,2,1536]{2,1,0:T(2,128)(2,1)S(1)}, u32[]{:S(2)}, u32[]{:S(2)}) async-start(bf16[128,2,1536]{2,1,0:T(2,128)(2,1)} %reshape.110), calls=%async_computation.2 | async-start | bytes 1572864 | tf_op jit(solution)/shard_map/all_to_all | solution.py:70
Sparse Core Ops, SparseCore 0:
  10.1 34.2 all-gather.7
  46.5 30.3 all-gather.5
  79.0 30.3 all-gather.3
  120.6 30.0 reduce-scatter.9
  153.4 29.1 reduce-scatter.11
  185.9 29.1 reduce-scatter.7
where the time goes:
time: 223 us; the launch traced here: 222 us
  waiting for transfers between devices  111 us (50%)
  starting transfers between devices  48.4 us (22%)
  local copies, waits for them, and re-layouts  33.3 us (15%)
  between operations  14.4 us (6%)
  matrix products  12.9 us (6%)
  other arithmetic  2.39 us (1%)
    all_gather x1, waiting for transfers between devices, shards(): lax.all_gather(w_down, 'dp', axis=1, tiled=True)  30.6 us
    all_to_all x1, waiting for transfers between devices, shards(): lax.all_to_all(send_rows, 'expert', split_axis=0, concat_axis=0, tiled=True)  24.8 us
    all_to_all x1, waiting for transfers between devices, shards(): lax.all_to_all(row_grad.reshape(experts_here, capacity, width), 'expert',...  23.5 us
    unnamed x27, local copies, waits for them, and re-layouts  23.2 us
    reduce_scatter x1, waiting for transfers between devices, shards(): lax.psum_scatter(part_down[None].astype(jnp.bfloat16), 'dp', scatter_dime...  17.7 us
    all_to_all x1, starting transfers between devices, shards(): lax.all_to_all(send_prob.astype(jnp.bfloat16), 'expert', split_axis=0, co...  17.4 us
    all_to_all x1, starting transfers between devices, shards(): lax.all_to_all(row_prob.reshape(experts_here, capacity).astype(jnp.bfloat...  14.2 us
    all_to_all x1, starting transfers between devices, shards(): lax.all_to_all(row_grad.reshape(experts_here, capacity, width), 'expert',...  10.1 us
  transfers between devices with their start and end apart: 10, of which 7 were waited for; matrix products, arithmetic and copies ran while one was open for 16% of the time, Pallas kernels for 0%

commit v1 on v0

--- a/solution.py
+++ b/solution.py
@@ -4,6 +4,18 @@
 from jax.sharding import PartitionSpec as P
 
 TOP = 8
+
+
+def gather_by_bits(x, axis, dim):
+    ways, here, lap = (lax.axis_size(axis), lax.axis_index(axis), x.shape[dim])
+    line, have = (x, 1)
+    while have < ways:
+        line = jnp.concatenate(
+            [line, lax.ppermute(line, axis, [(d, (d - have) % ways) for d in range(ways)])],
+            axis=dim,
+        )
+        have = 2 * have
+    return jnp.roll(line, here * lap, axis=dim)
 
 
 def expert_rows(inputs_rows, grad_rows, prob, gate_w, up_w, down_w):
@@ -52,7 +64,7 @@
     gathered = (
         lax.all_gather(w_gate, "dp", axis=1, tiled=True),
         lax.all_gather(w_up, "dp", axis=1, tiled=True),
-        lax.all_gather(w_down, "dp", axis=1, tiled=True),
+        gather_by_bits(w_down, "dp", 1),
     )
     gate_w = gathered[0][0]
     up_w = gathered[1][0]

time: 223 us -> 207 us (0.928)
  waiting for transfers between devices: 111 us -> 83.5 us
  starting transfers between devices: 48.4 us -> 56.7 us
  local copies, waits for them, and re-layouts: 33.3 us -> 36.9 us
    all_gather x1 -> x0, waiting for transfers between devices: 30.6 us -> none  [shards(): lax.all_gather(w_down, 'dp', axis=1, tiled=True)]
    ppermute x0 -> x2, waiting for transfers between devices: none -> 26.2 us  [gather_by_bits(): lax.ppermute(line, axis, [(d, (d - have) % ways) for d in range(ways)])]
    all_to_all x1, waiting for transfers between devices: 24.8 us -> 0.01 us  [shards(): lax.all_to_all(send_rows, 'expert', split_axis=0, concat_axis=0, tiled=True)]
    ppermute x0 -> x2, starting transfers between devices: none -> 9.32 us  [gather_by_bits(): lax.ppermute(line, axis, [(d, (d - have) % ways) for d in range(ways)])]
    reduce_scatter x1, waiting for transfers between devices: 17.7 us -> 20.8 us  [shards(): lax.psum_scatter(part_down[None].astype(jnp.bfloat16), 'dp', scatter_dime...]
    unnamed x27 -> x32, local copies, waits for them, and re-layouts: 23.2 us -> 25.9 us
  transfers between devices with their start and end apart: 10 -> 11, of which waited for: 7 -> 6; matrix products, arithmetic and copies ran while one was open for 16% -> 19% of each run, Pallas kernels for 0% -> 0%
where the time goes in v1:
time: 207 us; the launch traced here: 206 us
  waiting for transfers between devices  83.5 us (40%)
  starting transfers between devices  56.7 us (27%)
  local copies, waits for them, and re-layouts  36.9 us (18%)
  between operations  14.1 us (7%)
  matrix products  12.3 us (6%)
  other arithmetic  2.45 us (1%)
    ppermute x2, waiting for transfers between devices, gather_by_bits(): lax.ppermute(line, axis, [(d, (d - have) % ways) for d in range(ways)])  26.2 us
    unnamed x32, local copies, waits for them, and re-layouts  25.9 us
    all_to_all x1, waiting for transfers between devices, shards(): lax.all_to_all(row_grad.reshape(experts_here, capacity, width), 'expert',...  23.5 us
    reduce_scatter x1, waiting for transfers between devices, shards(): lax.psum_scatter(part_down[None].astype(jnp.bfloat16), 'dp', scatter_dime...  20.8 us
    all_to_all x1, starting transfers between devices, shards(): lax.all_to_all(send_prob.astype(jnp.bfloat16), 'expert', split_axis=0, co...  17.4 us
    all_to_all x1, starting transfers between devices, shards(): lax.all_to_all(row_prob.reshape(experts_here, capacity).astype(jnp.bfloat...  13.9 us
    all_to_all x1, starting transfers between devices, shards(): lax.all_to_all(row_grad.reshape(experts_here, capacity, width), 'expert',...  9.34 us
    ppermute x2, starting transfers between devices, gather_by_bits(): lax.ppermute(line, axis, [(d, (d - have) % ways) for d in range(ways)])  9.32 us
  transfers between devices with their start and end apart: 11, of which 6 were waited for; matrix products, arithmetic and copies ran while one was open for 19% of the time, Pallas kernels for 0%

profile of v1, /device:TPU:8, one launch (start us, length us, event | category | flops | bytes accessed | tf_op | source)
XLA Modules:
  0.0 206.0 jit_solution(12360988327982881482)
XLA Ops:
  10.9 1.0 scatter_custom_fusion
  12.7 17.4 %all-to-all-start = ((bf16[128,1,2]{2,1,0:T(2,128)(2,1)}), bf16[128,1,2]{2,1,0:T(2,128)(2,1)S(1)}, u32[]{:S(2)}, u32[]{:S(2)}) async-start(bf16[128,1,2]{2,1,0:T(2,128)(2,1)} %convert_element_type.113), calls=%async_computation | async-start | bytes 131072 | tf_op jit(solution)/shard_map/all_to_all | solution.py:60
  30.1 1.7 scatter_custom_fusion.1
  31.9 1.2 reshape.108
  33.0 7.8 %all-to-all-done = bf16[128,1,2]{2,1,0:T(2,128)(2,1)S(1)} async-done(((bf16[128,1,2]{2,1,0:T(2,128)(2,1)}), bf16[128,1,2]{2,1,0:T(2,128)(2,1)S(1)}, u32[]{:S(2)}, u32[]{:S(2)}) %all-to-all-start) | async-done | bytes 544 | tf_op jit(solution)/shard_map/all_to_all | solution.py:60
  40.9 6.5 %all-to-all-start.1 = ((bf16[128,2,1536]{2,1,0:T(2,128)(2,1)}), bf16[128,2,1536]{2,1,0:T(2,128)(2,1)S(1)}, u32[]{:S(2)}, u32[]{:S(2)}) async-start(bf16[128,2,1536]{2,1,0:T(2,128)(2,1)} %reshape.108), calls=%async_computation.1 | async-start | bytes 1572864 | tf_op jit(solution)/shard_map/all_to_all | solution.py:59
  47.4 4.7 %collective-permute-start = (bf16[1,384,384]{2,1,0:T(8,128)(2,1)S(1)}, bf16[1,384,384]{2,1,0:T(8,128)(2,1)S(1)}, u32[]{:S(2)}, u32[]{:S(2)}) collective-permute-start(bf16[1,384,384]{2,1,0:T(8,128)(2,1)S(1)} %copy-done.3), channel_id=1, source_target_pairs={{0,384},{128,0},{256,128},{384,256},{1,385},{129,1},{257,129},{385... | collective-permute-start | bytes 884744 | tf_op jit(solution)/shard_map/ppermute | solution.py:14
  52.2 6.5 %collective-permute-done = bf16[1,384,384]{2,1,0:T(8,128)(2,1)S(1)} collective-permute-done((bf16[1,384,384]{2,1,0:T(8,128)(2,1)S(1)}, bf16[1,384,384]{2,1,0:T(8,128)(2,1)S(1)}, u32[]{:S(2)}, u32[]{:S(2)}) %collective-permute-start) | collective-permute-done | bytes 294944 | tf_op jit(solution)/shard_map/ppermute | solution.py:14
  58.7 4.7 %collective-permute-start.1 = (bf16[1,768,384]{2,1,0:T(8,128)(2,1)S(1)}, bf16[1,768,384]{2,1,0:T(8,128)(2,1)S(1)}, u32[]{:S(2)}, u32[]{:S(2)}) collective-permute-start(bf16[1,768,384]{2,1,0:T(8,128)(2,1)S(1)} %pad_maximum_fusion), channel_id=1, source_target_pairs={{0,256},{128,384},{256,0},{384,128},{1,257},{129,385},{257,1},{385... | collective-permute-start | bytes 1769480 | tf_op jit(solution)/shard_map/ppermute | solution.py:14
  65.2 19.7 %collective-permute-done.1 = bf16[1,768,384]{2,1,0:T(8,128)(2,1)S(1)} collective-permute-done((bf16[1,768,384]{2,1,0:T(8,128)(2,1)S(1)}, bf16[1,768,384]{2,1,0:T(8,128)(2,1)S(1)}, u32[]{:S(2)}, u32[]{:S(2)}) %collective-permute-start.1) | collective-permute-done | bytes 589856 | tf_op jit(solution)/shard_map/ppermute | solution.py:14
  84.9 0.9 constant_dynamic-update-slice_fusion.3
  87.3 0.9 constant_dynamic-update-slice_fusion
  88.6 2.1 %fusion.6 = f32[256,384]{1,0:T(8,128)S(1)} fusion(bf16[1,1536,384]{2,1,0:T(8,128)(2,1)} %all-gather.5.cloned.1.call-done, bf16[1,1,256,1536]{3,2,1,0:T(8,128)(2,1)S(1)} %copy-done), kind=kOutput, calls=%fused_computation.16 | convolution fusion | flops 301989888 | bytes 2359296 | tf_op jit(solution)/shard_map/dot_general | solution.py:22
  90.7 2.0 fusion.9
  93.7 1.5 fusion.1
  95.2 6.3 %copy.32 = bf16[1,1536,384]{2,0,1:T(2,128)(2,1)S(1)} copy(bf16[1,1536,384]{1,2,0:T(8,128)(2,1)} %fusion.1) | data formatting | bytes 2359296
  101.5 1.2 copy.43
  102.7 1.5 fusion.2
  104.3 6.3 %copy.34 = bf16[1,1536,384]{2,0,1:T(2,128)(2,1)S(1)} copy(bf16[1,1536,384]{1,2,0:T(8,128)(2,1)} %fusion.2) | data formatting | bytes 2359296
  110.5 1.2 copy.42
  112.6 13.9 %all-to-all-start.3 = ((bf16[128,1,2]{2,1,0:T(2,128)(2,1)}), bf16[128,1,2]{2,1,0:T(2,128)(2,1)S(1)}, u32[]{:S(2)}, u32[]{:S(2)}) async-start(bf16[128,1,2]{2,1,0:T(2,128)(2,1)} %convert_element_type.114), calls=%async_computation.3 | async-start | bytes 131072 | tf_op jit(solution)/shard_map/all_to_all | solution.py:89
  126.6 3.2 %fusion.3 = bf16[1,1536,384]{2,1,0:T(8,128)(2,1)} fusion(bf16[256,1536]{1,0:T(8,128)(2,1)} %copy-done.4, f32[256]{0:T(256)S(1)} %reshape.114, f32[256,384]{1,0:T(8,128)} %copy-done.6, f32[256,384]{1,0:T(8,128)} %copy-done.5), kind=kOutput, calls=%fused_computation.11 | convolution fusion | flops 303267840 | bytes 2753536 | tf_op jit(solution)/shard_map/dot_general | solution.py:80
  131.7 1.2 reshape.110
  132.9 4.4 %all-to-all-done.3 = bf16[128,1,2]{2,1,0:T(2,128)(2,1)S(1)} async-done(((bf16[128,1,2]{2,1,0:T(2,128)(2,1)}), bf16[128,1,2]{2,1,0:T(2,128)(2,1)S(1)}, u32[]{:S(2)}, u32[]{:S(2)}) %all-to-all-start.3) | async-done | bytes 544 | tf_op jit(solution)/shard_map/all_to_all | solution.py:89
  137.3 9.3 %all-to-all-start.2 = ((bf16[128,2,1536]{2,1,0:T(2,128)(2,1)}), bf16[128,2,1536]{2,1,0:T(2,128)(2,1)S(1)}, u32[]{:S(2)}, u32[]{:S(2)}) async-start(bf16[128,2,1536]{2,1,0:T(2,128)(2,1)} %reshape.110), calls=%async_computation.2 | async-start | bytes 1572864 | tf_op jit(solution)/shard_map/all_to_all | solution.py:82
  147.0 1.3 gather_fusion.1
  149.1 23.5 %all-to-all-done.2 = bf16[128,2,1536]{2,1,0:T(2,128)(2,1)S(1)} async-done(((bf16[128,2,1536]{2,1,0:T(2,128)(2,1)}), bf16[128,2,1536]{2,1,0:T(2,128)(2,1)S(1)}, u32[]{:S(2)}, u32[]{:S(2)}) %all-to-all-start.2) | async-done | bytes 786464 | tf_op jit(solution)/shard_map/all_to_all | solution.py:82
  172.8 0.9 gather_fusion
  173.7 0.9 bitcast_reduce_fusion
  174.6 1.3 reshape_bitcast_fusion.1
  176.6 1.3 reshape_bitcast_fusion
  178.7 20.8 %reduce-scatter.8.cloned.1.call-done = bf16[1,384,384]{2,1,0:T(8,128)(2,1)} async-done(((bf16[1,1536,384]{2,1,0:T(8,128)(2,1)}), bf16[1,384,384]{2,1,0:T(8,128)(2,1)}) %reduce-scatter.8.cloned.1.call-update) | async-done | bytes 294928 | tf_op jit(solution)/shard_map/reduce_scatter | solution.py:109
  (64 shorter events, 14.9 us)
Async XLA Ops:
  7.2 81.4 %copy-start = (bf16[1,1,256,1536]{3,2,1,0:T(8,128)(2,1)S(1)}, bf16[1,1,256,1536]{3,2,1,0:T(8,128)(2,1)}, u32[]{:S(2)}) copy-start(bf16[1,1,256,1536]{3,2,1,0:T(8,128)(2,1)} %param.10) | copy-start | bytes 2359300
  7.2 81.4 %all-gather.5.cloned.1.call-start = ((), (), s32[]{:S(2)}) async-start(), calls=%async_computation.8 | async-start | bytes 1474560 | tf_op jit(solution)/shard_map/all_gather | solution.py:65
  12.7 28.1 %all-to-all-start = ((bf16[128,1,2]{2,1,0:T(2,128)(2,1)}), bf16[128,1,2]{2,1,0:T(2,128)(2,1)S(1)}, u32[]{:S(2)}, u32[]{:S(2)}) async-start(bf16[128,1,2]{2,1,0:T(2,128)(2,1)} %convert_element_type.113), calls=%async_computation | async-start | bytes 131072 | tf_op jit(solution)/shard_map/all_to_all | solution.py:60
  31.8 15.6 %copy-start.3 = (bf16[1,384,384]{2,1,0:T(8,128)(2,1)S(1)}, bf16[1,384,384]{2,1,0:T(8,128)(2,1)}, u32[]{:S(2)}) copy-start(bf16[1,384,384]{2,1,0:T(8,128)(2,1)} %param.13) | copy-start | bytes 884740
  40.9 47.3 %all-to-all-start.1 = ((bf16[128,2,1536]{2,1,0:T(2,128)(2,1)}), bf16[128,2,1536]{2,1,0:T(2,128)(2,1)S(1)}, u32[]{:S(2)}, u32[]{:S(2)}) async-start(bf16[128,2,1536]{2,1,0:T(2,128)(2,1)} %reshape.108), calls=%async_computation.1 | async-start | bytes 1572864 | tf_op jit(solution)/shard_map/all_to_all | solution.py:59
  47.4 43.3 %all-gather.3.cloned.1.call-start = ((), (), s32[]{:S(2)}) async-start(), calls=%async_computation.7 | async-start | bytes 1474560 | tf_op jit(solution)/shard_map/all_gather | solution.py:66
  47.4 11.2 %collective-permute-start = (bf16[1,384,384]{2,1,0:T(8,128)(2,1)S(1)}, bf16[1,384,384]{2,1,0:T(8,128)(2,1)S(1)}, u32[]{:S(2)}, u32[]{:S(2)}) collective-permute-start(bf16[1,384,384]{2,1,0:T(8,128)(2,1)S(1)} %copy-done.3), channel_id=1, source_target_pairs={{0,384},{128,0},{256,128},{384,256},{1,385},{129,1},{257,129},{385... | collective-permute-start | bytes 884744 | tf_op jit(solution)/shard_map/ppermute | solution.py:14
  52.1 122.5 %reduce-scatter.10.cloned.1.call-start = ((), (), s32[]{:S(2)}) async-start(), calls=%async_computation.10 | async-start | bytes 1474560
  58.7 26.2 %collective-permute-start.1 = (bf16[1,768,384]{2,1,0:T(8,128)(2,1)S(1)}, bf16[1,768,384]{2,1,0:T(8,128)(2,1)S(1)}, u32[]{:S(2)}, u32[]{:S(2)}) collective-permute-start(bf16[1,768,384]{2,1,0:T(8,128)(2,1)S(1)} %pad_maximum_fusion), channel_id=1, source_target_pairs={{0,256},{128,384},{256,0},{384,128},{1,257},{129,385},{257,1},{385... | collective-permute-start | bytes 1769480 | tf_op jit(solution)/shard_map/ppermute | solution.py:14
  88.5 4.2 %copy-start.4 = (bf16[256,1536]{1,0:T(8,128)(2,1)}, bf16[256,1536]{1,0:T(8,128)(2,1)S(1)}, u32[]{:S(2)}) copy-start(bf16[256,1536]{1,0:T(8,128)(2,1)S(1)} %reshape.109) | copy-start | bytes 2359300
  90.7 3.0 %copy-start.5 = (f32[256,384]{1,0:T(8,128)}, f32[256,384]{1,0:T(8,128)S(1)}, u32[]{:S(2)}) copy-start(f32[256,384]{1,0:T(8,128)S(1)} %fusion.6) | copy-start | bytes 1179652
  90.7 2.1 %copy-start.7 = (bf16[1,3072,384]{2,1,0:T(8,128)(2,1)S(1)}, bf16[1,3072,384]{2,1,0:T(8,128)(2,1)}, u32[]{:S(2)}) copy-start(bf16[1,3072,384]{2,1,0:T(8,128)(2,1)} %constant_dynamic-update-slice_fusion) | copy-start | bytes 7077892
  92.9 0.8 copy-start.6
  102.7 74.0 %reduce-scatter.12.cloned.1.call-start = ((), (), s32[]{:S(2)}) async-start(), calls=%async_computation.11 | async-start | bytes 1474560
  112.6 24.7 %all-to-all-start.3 = ((bf16[128,1,2]{2,1,0:T(2,128)(2,1)}), bf16[128,1,2]{2,1,0:T(2,128)(2,1)S(1)}, u32[]{:S(2)}, u32[]{:S(2)}) async-start(bf16[128,1,2]{2,1,0:T(2,128)(2,1)} %convert_element_type.114), calls=%async_computation.3 | async-start | bytes 131072 | tf_op jit(solution)/shard_map/all_to_all | solution.py:89
  126.6 3.3 %copy-start.2 = (bf16[1,1536,384]{2,1,0:T(8,128)(2,1)S(1)}, bf16[1,1536,384]{2,1,0:T(8,128)(2,1)}, u32[]{:S(2)}) copy-start(bf16[1,1536,384]{2,1,0:T(8,128)(2,1)} %all-gather.5.cloned.1.call-done) | copy-start | bytes 3538948
  126.6 72.9 %reduce-scatter.8.cloned.1.call-start = ((), (), s32[]{:S(2)}) async-start(), calls=%async_computation.9 | async-start | bytes 1474560 | tf_op jit(solution)/shard_map/reduce_scatter | solution.py:109
  129.8 1.3 copy-start.1
  137.3 35.2 %all-to-all-start.2 = ((bf16[128,2,1536]{2,1,0:T(2,128)(2,1)}), bf16[128,2,1536]{2,1,0:T(2,128)(2,1)S(1)}, u32[]{:S(2)}, u32[]{:S(2)}) async-start(bf16[128,2,1536]{2,1,0:T(2,128)(2,1)} %reshape.110), calls=%async_computation.2 | async-start | bytes 1572864 | tf_op jit(solution)/shard_map/all_to_all | solution.py:82
Sparse Core Ops, SparseCore 0:
  10.1 34.3 all-gather.4
  52.3 34.8 all-gather.2
  102.8 32.2 reduce-scatter.9
  137.8 29.1 reduce-scatter.11
  170.3 29.1 reduce-scatter.7
